TPU v7x, 32 devices: a whole 2x2x4 slice. The times are simulated.
32 devices in a mesh: groups: 2 (over y), ctx: 4 (over z), chan: 4 (over x, core).
Axes of the slice: x: 2, y: 2, z: 4, core: 2. Of those that a mesh axis runs over, the one named last changes fastest.
Arguments:
- projected: bfloat16 [3, 2048, 4096], P(None, ('groups', 'ctx'), 'chan'), parts along dimension 1, may hold values from -6 to 6
- short_filter: float32 [3, 3, 4096], P(None, None, 'chan'), may hold values from -3 to 3
- decay_rates: float32 [16, 4096], P(None, 'chan'), may hold values from 0.0001953125 to 0.05
- residues: float32 [16, 4096], P(None, 'chan'), may hold values from -1.5 to 1.5
- skip_gain: float32 [4096], P('chan'), may hold values from -4 to 4
- out_weight: bfloat16 [4096, 2048], P('chan'), may hold values from -0.09375 to 0.09375
Outputs:
- layer_out: bfloat16 [2048, 2048], P(('groups', 'ctx'), 'chan'), parts along dimension 0
There are 2 independent parts, one for each index of `groups`. A program takes and returns all parts, laid end to end along the dimension named above; an argument that names none is the same for every part. Nothing has to cross between parts.
All inputs are finite; a program needn't handle non-finite values.
Results may differ from a plain program's by a relative error of at most 0.012.
Values may be sent and summed in bfloat16 or wider, within the bound.
A program may use at most 128 MiB of HBM per device.

v0:
```python
import math

import jax
import jax.numpy as jnp
from jax import lax
from jax.sharding import PartitionSpec as P


def from_behind(value, axis, steps):
    count = lax.axis_size(axis)
    first, last = (max(0, -steps), min(count, count - steps))
    return lax.ppermute(value, axis, [(source, source + steps) for source in range(first, last)])


def prefix(value, axis, join, neutral):
    count, mine = (lax.axis_size(axis), lax.axis_index(axis))
    pieces = jax.tree.map(lambda part: lax.all_gather(part, axis), value)
    running = jax.tree.map(
        lambda part, zero: jnp.full_like(part, 0) + jnp.asarray(zero, part.dtype), value, neutral
    )

    def lap(position, running):
        longer = join(running, jax.tree.map(lambda part: part[position], pieces))
        return jax.tree.map(lambda new, old: jnp.where(position < mine, new, old), longer, running)

    return lax.fori_loop(0, count - 1, lap, running)


def fourier_tables(length):
    double = 2 * length
    freq = lax.broadcasted_iota(jnp.int32, (double, length), 0)
    places = lax.broadcasted_iota(jnp.int32, (double, length), 1)
    phase = (freq * places % double).astype(jnp.float32) * (2.0 * math.pi / double)
    return (jnp.cos(phase), jnp.sin(phase))


def forward_product(table, signal):
    return jnp.dot(
        table, signal, precision=lax.Precision.HIGHEST, preferred_element_type=jnp.float32
    )


def inverse_product(table, spectrum):
    return lax.dot_general(
        table,
        spectrum,
        (((0,), (0,)), ((), ())),
        precision=lax.Precision.HIGHEST,
        preferred_element_type=jnp.float32,
    )


def local_convolve(signal, filt):
    length, width_dev = signal.shape
    cos_table, sin_table = fourier_tables(length)
    stacked = jnp.concatenate([signal, filt], axis=1)
    cos_part = forward_product(cos_table, stacked)
    sin_part = forward_product(sin_table, stacked)
    sig_cos, fil_cos = (cos_part[:, :width_dev], cos_part[:, width_dev:])
    sig_sin, fil_sin = (sin_part[:, :width_dev], sin_part[:, width_dev:])
    real_part = sig_cos * fil_cos - sig_sin * fil_sin
    imag_part = -(sig_cos * fil_sin + sig_sin * fil_cos)
    result = inverse_product(cos_table, real_part) - inverse_product(sin_table, imag_part)
    return result / (2.0 * length)


def body(projected, short_filter, decay_rates, residues, skip_gain, out_weight):
    length = projected.shape[1]
    edges = from_behind(projected[:, length - 2 :, :], "ctx", 1)
    extended = jnp.concatenate([edges, projected], axis=1).astype(jnp.float32)
    mixed = short_filter[:, 0, None, :] * extended[:, 2:, :]
    mixed = mixed + short_filter[:, 1, None, :] * extended[:, 1:-1, :]
    mixed = mixed + short_filter[:, 2, None, :] * extended[:, :-2, :]
    query = mixed[0]
    gated = (mixed[1] * mixed[2]).astype(jnp.bfloat16)
    gated_f = gated.astype(jnp.float32)
    scaled = residues * jnp.sqrt(-jnp.expm1(-2.0 * decay_rates))
    offsets = jnp.arange(length, dtype=jnp.float32)
    decays = jnp.exp(-decay_rates[None, :, :] * offsets[:, None, None])
    filt = jnp.sum(decays * scaled[None, :, :], axis=1)
    nearby = local_convolve(gated_f, filt)
    own_state = jnp.sum(decays[::-1] * gated_f[:, None, :], axis=0)
    passing = jnp.exp(-decay_rates * length)

    def combine(earlier, later):
        return (later[0] + later[1] * earlier[0], earlier[1] * later[1])

    identity = (jnp.zeros(decay_rates.shape, jnp.float32), jnp.ones(decay_rates.shape, jnp.float32))
    carried, unused_decay = prefix((own_state, passing), "ctx", combine, identity)
    step_decay = jnp.exp(-decay_rates)
    distant = jnp.sum(decays * (step_decay * scaled * carried)[None, :, :], axis=1)
    mixed_out = (query * (nearby + distant + skip_gain[None, :] * gated_f)).astype(jnp.bfloat16)
    columns = lax.all_to_all(out_weight, "chan", split_axis=1, concat_axis=0, tiled=True)
    totals = jnp.dot(
        lax.all_gather(mixed_out, "chan", axis=1, tiled=True),
        columns,
        preferred_element_type=jnp.float32,
    )
    return totals.astype(jnp.bfloat16)


def solution(mesh):
    in_specs = (
        P(None, ("groups", "ctx"), "chan"),
        P(None, None, "chan"),
        P(None, "chan"),
        P(None, "chan"),
        P("chan"),
        P("chan", None),
    )
    out_specs = P(("groups", "ctx"), "chan")
    return jax.shard_map(body, mesh=mesh, in_specs=in_specs, out_specs=out_specs, check_vma=False)
```

profile of v0, /device:TPU:0, one launch (start us, length us, event | category | flops | bytes accessed | tf_op | source)
XLA Modules:
  0.0 135.5 jit_solution(17840227853066893665)
XLA Ops:
  6.5 0.8 slice.43
  7.4 4.9 %collective-permute-start = (bf16[3,2,1024]{2,1,0:T(2,128)(2,1)S(1)}, bf16[3,2,1024]{2,1,0:T(2,128)(2,1)S(1)}, u32[]{:S(2)}, u32[]{:S(2)}) collective-permute-start(bf16[3,2,1024]{2,1,0:T(2,128)(2,1)S(1)} %slice.43), channel_id=1, source_target_pairs={{0,4},{4,8},{8,12},{1,5},{5,9},{9,13},{2,6},{6,10},{10,14},{3,7},{... | collective-permute-start | bytes 36872 | tf_op jit(solution)/shard_map/ppermute | solution.py:12
  12.3 6.4 %copy.9 = bf16[1024,2048]{0,1:T(8,128)(2,1)} copy(bf16[1024,2048]{1,0:T(8,128)(2,1)} %param.13) | data formatting | bytes 8388608 | tf_op args[5]
  18.7 5.0 %all-to-all-start = ((bf16[1024,4,512]{0,2,1:T(8,128)(2,1)}), bf16[1024,4,512]{0,2,1:T(8,128)(2,1)}, u32[]{:S(2)}, u32[]{:S(2)}) async-start(bf16[1024,4,512]{0,2,1:T(8,128)(2,1)} %bitcast.37), calls=%async_computation | async-start | bytes 8388608 | tf_op jit(solution)/shard_map/all_to_all | solution.py:93
  23.7 0.0 all-gather.4.cloned.1.call-start
  23.9 7.9 %multiply_exponential_fusion = f32[256,16,1024]{2,1,0:T(8,128)} fusion(f32[16,1024]{1,0:T(8,128)S(1)} %get-tuple-element.133), kind=kLoop, calls=%fused_computation.6 | loop fusion | flops 4194304 | bytes 16842752 | tf_op jit(solution)/shard_map/exp | solution.py:79
  31.8 14.3 %all-gather.1 = f32[64,1024]{1,0:T(8,128)S(1)} all-gather(f32[16,1024]{1,0:T(8,128)S(1)} %get-tuple-element.132), channel_id=3, replica_groups=mesh['groups'=2,'ctx'=4,'chan'=4] {'ctx'}, dimensions={0}, use_global_device_ids=true | all-gather | bytes 327680 | tf_op jit(solution)/shard_map/all_gather | solution.py:17
  46.1 0.5 maximum_convert_fusion
  46.6 0.9 fusion.2
  47.5 1.7 %copy-done = f32[3,256,1024]{2,1,0:T(8,128)} copy-done((f32[3,256,1024]{2,1,0:T(8,128)}, f32[3,256,1024]{2,1,0:T(8,128)S(1)}, u32[]{:S(2)}) %copy-start) | copy-done | bytes 3145752
  49.3 0.1 fusion.44
  49.4 7.4 %multiply_reduce_fusion.1 = f32[16,1024]{1,0:T(8,128)S(1)} fusion(f32[256,16,1024]{2,1,0:T(8,128)} %multiply_exponential_fusion, f32[256,1024]{1,0:T(8,128)S(1)} %fusion.44), kind=kLoop, calls=%fused_computation.4 | loop fusion | flops 8372224 | bytes 17891328 | tf_op jit(solution)/shard_map/reduce_sum | solution.py:82
  56.8 13.8 %all-gather = f32[64,1024]{1,0:T(8,128)S(1)} all-gather(f32[16,1024]{1,0:T(8,128)S(1)} %multiply_reduce_fusion.1), channel_id=2, replica_groups=mesh['groups'=2,'ctx'=4,'chan'=4] {'ctx'}, dimensions={0}, use_global_device_ids=true | all-gather | bytes 327680 | tf_op jit(solution)/shard_map/all_gather | solution.py:17
  70.6 0.1 while.14
  70.7 0.1 multiply_multiply_fusion
  70.8 9.2 %multiply_reduce_fusion.2 = (f32[256,1024]{1,0:T(8,128)S(1)}, f32[256,1024]{1,0:T(8,128)S(1)}) fusion(f32[16,1024]{1,0:T(8,128)S(1)} %get-tuple-element.131, f32[16,1024]{1,0:T(8,128)S(1)} %get-tuple-element.133, f32[16,1024]{1,0:T(8,128)S(1)} %get-tuple-element.130), kind=kLoop, calls=%fused_computation.5 | loop fusion | flops 20447232 | bytes 2293760 | tf_op jit(solution)/shard_map/reduce_sum | solution.py:80
  80.0 5.4 %fusion.22 = f32[512,2048]{1,0:T(8,128)S(1)} fusion(f32[256,1024]{1,0:T(8,128)S(1)} %get-tuple-element.118, f32[256,1024]{1,0:T(8,128)S(1)} %fusion.44), kind=kOutput, calls=%fused_computation.31 | convolution fusion | flops 3223584768 | bytes 6291456 | tf_op jit(solution)/shard_map/dot_general | solution.py:38
  85.4 5.4 %fusion.21 = f32[512,2048]{1,0:T(8,128)S(1)} fusion(f32[256,1024]{1,0:T(8,128)S(1)} %get-tuple-element.118, f32[256,1024]{1,0:T(8,128)S(1)} %fusion.44), kind=kOutput, calls=%fused_computation.30 | convolution fusion | flops 3223584768 | bytes 6291456 | tf_op jit(solution)/shard_map/dot_general | solution.py:38
  90.9 4.3 %fusion.4 = f32[256,1024]{1,0:T(8,128)S(1)} fusion(f32[512,2048]{1,0:T(8,128)S(1)} %fusion.21, f32[512,2048]{1,0:T(8,128)S(1)} %fusion.22), kind=kOutput, calls=%fused_computation.13 | convolution fusion | flops 1614544896 | bytes 9437184 | tf_op jit(solution)/shard_map/dot_general | solution.py:44
  95.2 6.2 %fusion.37 = bf16[256,1024]{1,0:T(8,128)(2,1)} fusion(f32[3,256,1024]{2,1,0:T(8,128)} %copy-done, f32[256,1024]{1,0:T(8,128)S(1)} %fusion.44, f32[256,1024]{1,0:T(8,128)S(1)} %get-tuple-element.119, f32[256,1024]{1,0:T(8,128)S(1)} %fusion.4, f32[512,2048]{1,0:T(8,128)S(1)} %fusion.21, f32[512,2048]{1,0:T(8,128)S(1)} %fusion.22, f32[1024]{0:T(1024)S(1)} %copy-done.5), kind=kOutput, calls=%fused_computation.42 | convolution fusion | flops 1615855616 | bytes 13111296 | tf_op jit(solution)/shard_map/dot_general | solution.py:44
  101.4 0.0 all-gather.4.cloned.1.call-update
  101.5 6.2 %copy.10 = bf16[4,1024,512]{2,1,0:T(8,128)(2,1)} copy(bf16[4,1024,512]{1,2,0:T(8,128)(2,1)} %bitcast.6) | data formatting | bytes 8388608 | tf_op jit(solution)/shard_map/all_to_all | solution.py:93
  107.7 16.2 %all-gather.4.cloned.1.call-done = bf16[256,4096]{1,0:T(8,128)(2,1)} async-done(((bf16[256,1024]{1,0:T(8,128)(2,1)}), bf16[256,4096]{1,0:T(8,128)(2,1)}) %all-gather.4.cloned.1.call-update) | async-done | bytes 2097168 | tf_op jit(solution)/shard_map/all_gather | solution.py:95
  123.9 4.8 %convolution_convert_fusion = bf16[256,512]{1,0:T(8,128)(2,1)} fusion(bf16[256,4096]{1,0:T(8,128)(2,1)} %all-gather.4.cloned.1.call-done, bf16[4096,512]{1,0:T(8,128)(2,1)} %bitcast.38), kind=kOutput, calls=%fused_computation.37 | convolution fusion | flops 1073872896 | bytes 6553600 | tf_op jit(solution)/shard_map/dot_general | solution.py:94
  (21 shorter events, 0.1 us)
Async XLA Ops:
  7.4 38.8 %collective-permute-start = (bf16[3,2,1024]{2,1,0:T(2,128)(2,1)S(1)}, bf16[3,2,1024]{2,1,0:T(2,128)(2,1)S(1)}, u32[]{:S(2)}, u32[]{:S(2)}) collective-permute-start(bf16[3,2,1024]{2,1,0:T(2,128)(2,1)S(1)} %slice.43), channel_id=1, source_target_pairs={{0,4},{4,8},{8,12},{1,5},{5,9},{9,13},{2,6},{6,10},{10,14},{3,7},{... | collective-permute-start | bytes 36872 | tf_op jit(solution)/shard_map/ppermute | solution.py:12
  18.7 5.0 %copy-start.4 = (f32[3,3,1024]{2,1,0:T(4,128)S(1)}, f32[3,3,1024]{2,1,0:T(4,128)}, u32[]{:S(2)}) copy-start(f32[3,3,1024]{2,1,0:T(4,128)} %param.9) | copy-start | bytes 110596
  18.7 5.1 %copy-start.2 = (f32[16,1024]{1,0:T(8,128)S(1)}, f32[16,1024]{1,0:T(8,128)}, u32[]{:S(2)}) copy-start(f32[16,1024]{1,0:T(8,128)} %param.10) | copy-start | bytes 196612
  18.7 82.7 %all-to-all-start = ((bf16[1024,4,512]{0,2,1:T(8,128)(2,1)}), bf16[1024,4,512]{0,2,1:T(8,128)(2,1)}, u32[]{:S(2)}, u32[]{:S(2)}) async-start(bf16[1024,4,512]{0,2,1:T(8,128)(2,1)} %bitcast.37), calls=%async_computation | async-start | bytes 8388608 | tf_op jit(solution)/shard_map/all_to_all | solution.py:93
  23.7 100.1 %all-gather.4.cloned.1.call-start = ((), (), s32[]{:S(2)}) async-start(), calls=%async_computation.1 | async-start | bytes 2621440 | tf_op jit(solution)/shard_map/all_gather | solution.py:95
  23.8 22.3 %copy-start.1 = (bf16[3,256,1024]{2,1,0:T(8,128)(2,1)S(1)}, bf16[3,256,1024]{2,1,0:T(8,128)(2,1)}, u32[]{:S(2)}) copy-start(bf16[3,256,1024]{2,1,0:T(8,128)(2,1)} %param.8) | copy-start | bytes 4718596
  47.5 1.7 %copy-start = (f32[3,256,1024]{2,1,0:T(8,128)}, f32[3,256,1024]{2,1,0:T(8,128)S(1)}, u32[]{:S(2)}) copy-start(f32[3,256,1024]{2,1,0:T(8,128)S(1)} %fusion.2) | copy-start | bytes 9437188
  49.4 21.3 %copy-start.3 = (f32[16,1024]{1,0:T(8,128)S(1)}, f32[16,1024]{1,0:T(8,128)}, u32[]{:S(2)}) copy-start(f32[16,1024]{1,0:T(8,128)} %param.11) | copy-start | bytes 196612
  90.9 4.3 %copy-start.5 = (f32[1024]{0:T(1024)S(1)}, f32[1024]{0:T(1024)}, u32[]{:S(2)}) copy-start(f32[1024]{0:T(1024)} %param.12) | copy-start | bytes 12292
Sparse Core Ops, SparseCore 0:
  101.6 22.2 all-gather.3
where the time goes:
time: 136 us; the launch traced here: 135 us
  blocking collectives  28.1 us (21%)
  other arithmetic  26.2 us (19%)
  matrix products  26.1 us (19%)
  waiting for transfers between devices  16.2 us (12%)
  local copies, waits for them, and re-layouts  15.2 us (11%)
  between operations  13.6 us (10%)
  starting transfers between devices  9.94 us (7%)
    all_gather x2, blocking collectives, prefix(): pieces = jax.tree.map(lambda part: lax.all_gather(part, axis), value)  28.1 us
    all_gather x1, waiting for transfers between devices, body(): lax.all_gather(mixed_out, 'chan', axis=1, tiled=True)  16.2 us
    dot_general x2, matrix products, forward_product(): jnp.dot(table, signal, precision=lax.Precision.HIGHEST, preferred_element...  10.9 us
    dot_general x2, matrix products, inverse_product(): lax.dot_general(table, spectrum, (((0,), (0,)), ((), ())), precision=lax....  10.5 us
    reduce_sum x1, other arithmetic, body(): filt = jnp.sum(decays * scaled[None, :, :], axis=1)  9.19 us
    unnamed x15, local copies, waits for them, and re-layouts  8.2 us
    exp x1, other arithmetic, body(): decays = jnp.exp(-decay_rates[None, :, :] * offsets[:, None, None])  7.9 us
    reduce_sum x1, other arithmetic, body(): own_state = jnp.sum(decays[::-1] * gated_f[:, None, :], axis=0)  7.42 us
  transfers between devices with their start and end apart: 3, of which 1 were waited for; matrix products, arithmetic and copies ran while one was open for 44% of the time, Pallas kernels for 0%

commit v1 on v0

v1 whole, which is shorter than its diff:
```python
import functools

import jax
import jax.numpy as jnp
from jax import lax
from jax.experimental import pallas as pl
from jax.experimental.pallas import tpu as pltpu
from jax.sharding import PartitionSpec as P

MESH = pl.DeviceIdType.MESH
LANES = 128
SUB = 8
STEP = 16
CHUNKS = 2


def expm1(v):
    series = jnp.ones_like(v)
    for order in range(9, 1, -1):
        series = 1.0 + series * v * (1.0 / order)
    return jnp.where(v > -0.3, v * series, jnp.exp(v) - 1.0)


def rows(token, count=1):
    start = token * SUB
    if not isinstance(start, int):
        start = pl.multiple_of(start, SUB)
    return pl.ds(start, count * SUB)


def kernel(
    n, m, proj_hbm, sf_ref, dr_ref, re_ref, sg_ref, w_hbm, out_ref,
    proj, wv, sft, dec, res, skip, decay, gain, passing, first_pow,
    x, q, g, y, mo, own, arrived, carried, ss, sr, xs, xr, acc,
    proj_sem, w_sem, edge_sem, state_send, state_recv, sib_send, sib_recv, far_send, far_recv,
):
    length, width = proj.shape[1:]
    modes = dr_ref.shape[0]
    blocks = width // LANES
    half = m // 2
    out_w = out_ref.shape[1]
    part = length // CHUNKS
    z, c = lax.axis_index("ctx"), lax.axis_index("chan")
    hi, lo = c // 2, lax.rem(c, 2)
    sibling = hi * 2 + (1 - lo)

    def far(o):
        return lax.rem(hi + o, half) * 2 + lo

    barrier = pltpu.get_barrier_semaphore()
    for off in range(1, n):
        pl.semaphore_signal(barrier, inc=1, device_id={"ctx": lax.rem(z + off, n)}, device_id_type=MESH)
    pl.semaphore_signal(barrier, inc=1, device_id={"chan": sibling}, device_id_type=MESH)
    for o in range(1, half):
        pl.semaphore_signal(barrier, inc=1, device_id={"chan": far(o)}, device_id_type=MESH)

    proj_copy = pltpu.make_async_copy(proj_hbm, proj, proj_sem)
    proj_copy.start()

    def w_copy(o, who):
        target = lax.rem(hi + o, half) * 2 + (lo if who else 1 - lo)
        columns = pl.ds(pl.multiple_of(target * out_w, LANES), out_w)
        slot = 2 * o + who
        return pltpu.make_async_copy(w_hbm.at[:, columns], wv.at[slot], w_sem.at[slot])

    for o in range(half):
        for who in range(2):
            w_copy(o, who).start()

    if blocks < SUB:
        for buffer in (sft, dec, res, skip, x):
            buffer[...] = jnp.zeros_like(buffer)
    for j in range(blocks):
        lanes = pl.ds(j * LANES, LANES)
        dec[pl.ds(j, modes, stride=SUB), :] = dr_ref[:, lanes]
        res[pl.ds(j, modes, stride=SUB), :] = re_ref[:, lanes]
        skip[pl.ds(j, 1), :] = sg_ref[:, lanes]
        for comp in range(3):
            sft[pl.ds(comp * 3 * SUB + j, 3, stride=SUB), :] = sf_ref[comp, :, lanes]
    rate = dec[...]
    decay[...] = jnp.exp(-rate)
    gain[...] = res[...] * jnp.sqrt(-expm1(-2.0 * rate))
    passing[...] = jnp.exp(-rate * float(length))
    first_pow[...] = jnp.exp(-rate * float(length - 2))

    proj_copy.wait()

    @pl.loop(0, length // STEP)
    def _(i):
        t = pl.multiple_of(i * STEP, STEP)
        for comp in range(3):
            for j in range(blocks):
                piece = proj[comp, pl.ds(t, STEP), pl.ds(j * LANES, LANES)].astype(jnp.float32)
                x[comp, pl.ds((t + 2) * SUB + j, STEP, stride=SUB), :] = piece

    pl.semaphore_wait(barrier, (n - 1) + 1 + (half - 1))

    edge = pltpu.make_async_remote_copy(
        src_ref=x.at[:, pl.ds(length * SUB, 2 * SUB), :],
        dst_ref=x.at[:, pl.ds(0, 2 * SUB), :],
        send_sem=edge_sem.at[0],
        recv_sem=edge_sem.at[1],
        device_id={"ctx": lax.rem(z + 1, n)},
        device_id_type=MESH,
    )

    @pl.when(z < n - 1)
    def _():
        edge.start()

    def mode(ref, k):
        return ref[pl.ds(k * SUB, SUB), :]

    def mix(t, count):
        taps = [sft[pl.ds(k * SUB, SUB), :] for k in range(9)]

        def one(comp):
            total = None
            for lag in range(3):
                value = x[comp, rows(t + 2 - lag, count), :].reshape(count, SUB, LANES)
                value = taps[comp * 3 + lag][None] * value
                total = value if total is None else total + value
            return total

        q[rows(t, count), :] = one(0).reshape(count * SUB, LANES)
        gated = (one(1) * one(2)).astype(jnp.bfloat16).astype(jnp.float32)
        g[rows(t, count), :] = gated.reshape(count * SUB, LANES)
        return gated

    def horner(state, gated, count):
        for s in range(count):
            state = [mode(decay, k) * state[k] + gated[s] for k in range(modes)]
        return state

    state = horner([jnp.zeros((SUB, LANES), jnp.float32)] * modes, mix(2, SUB - 2), SUB - 2)

    def own_lap(i, state):
        return tuple(horner(list(state), mix(i * SUB, SUB), SUB))

    state = list(lax.fori_loop(1, length // SUB, own_lap, tuple(state)))

    @pl.when(z == 0)
    def _():
        x[:, pl.ds(0, 2 * SUB), :] = jnp.zeros((3, 2 * SUB, LANES), jnp.float32)

    @pl.when(z > 0)
    def _():
        edge.wait_recv()

    head = mix(0, 2)
    for k in range(0, modes, 2):
        pair = [
            state[k + e] + mode(first_pow, k + e) * (mode(decay, k + e) * head[0] + head[1]) for e in range(2)
        ]
        own[pl.ds(k * SUB, 2 * SUB), :] = jnp.concatenate(pair, axis=0).astype(jnp.bfloat16)

    def send_state(off):
        return pltpu.make_async_remote_copy(
            src_ref=own,
            dst_ref=arrived.at[off - 1],
            send_sem=state_send.at[off - 1],
            recv_sem=state_recv.at[off - 1],
            device_id={"ctx": lax.rem(z + off, n)},
            device_id_type=MESH,
        )

    for off in range(1, n):

        @pl.when(z + off < n)
        def _(off=off):
            send_state(off).start()

    def near_lap(i, state):
        state = list(state)
        for s in range(SUB):
            token = rows(i * SUB + s)
            gated = g[token, :]
            sums = [None] * 4
            for k in range(modes):
                state[k] = mode(decay, k) * state[k] + gated
                term = mode(gain, k) * state[k]
                sums[k % 4] = term if sums[k % 4] is None else sums[k % 4] + term
            y[token, :] = (sums[0] + sums[1]) + (sums[2] + sums[3])
        return tuple(state)

    lax.fori_loop(
        0, length // SUB, near_lap, tuple(jnp.zeros((SUB, LANES), jnp.float32) for _ in range(modes))
    )

    carried[...] = jnp.zeros_like(carried)
    for off in range(n - 1, 0, -1):

        @pl.when(z >= off)
        def _(off=off):
            send_state(off).wait_recv()
            carried[...] = carried[...] * passing[...] + arrived[off - 1].astype(jnp.float32)

    reach = [mode(carried, k) * mode(gain, k) * mode(decay, k) for k in range(modes)]

    def finish_lap(i, reach):
        reach = list(reach)
        for s in range(SUB):
            token = rows(i * SUB + s)
            total = y[token, :] + skip[...] * g[token, :]
            sums = [total, None, None, None]
            for k in range(modes):
                sums[k % 4] = reach[k] if sums[k % 4] is None else sums[k % 4] + reach[k]
                reach[k] = reach[k] * mode(decay, k)
            y[token, :] = q[token, :] * ((sums[0] + sums[1]) + (sums[2] + sums[3]))
        return tuple(reach)

    def gather_lap(i):
        t = pl.multiple_of(i * STEP, STEP)
        for j in range(blocks):
            piece = y[pl.ds(t * SUB + j, STEP, stride=SUB), :]
            mo[pl.ds(t, STEP), pl.ds(j * LANES, LANES)] = piece.astype(jnp.bfloat16)

    def to_sibling(o, p):
        return pltpu.make_async_remote_copy(
            src_ref=ss.at[o, p],
            dst_ref=sr.at[o, p],
            send_sem=sib_send.at[o, p],
            recv_sem=sib_recv.at[o, p],
            device_id={"chan": sibling},
            device_id_type=MESH,
        )

    def to_far(o, p):
        return pltpu.make_async_remote_copy(
            src_ref=xs.at[o - 1, p],
            dst_ref=xr.at[o - 1, p],
            send_sem=far_send.at[o - 1, p],
            recv_sem=far_recv.at[o - 1, p],
            device_id={"chan": far(o)},
            device_id_type=MESH,
        )

    def product(p, slot):
        return jnp.dot(mo[pl.ds(p * part, part), :], wv[slot], preferred_element_type=jnp.float32)

    order = list(range(1, half)) + [0]
    for p in range(CHUNKS):
        first, last = p * part // SUB, (p + 1) * part // SUB
        reach = list(lax.fori_loop(first, last, finish_lap, tuple(reach)))
        pl.loop(p * part // STEP, (p + 1) * part // STEP)(gather_lap)
        for o in order:
            if p == 0:
                w_copy(o, 0).wait()
            ss[o, p] = product(p, 2 * o).astype(jnp.bfloat16)
            to_sibling(o, p).start()
        for o in order:
            if p == 0:
                w_copy(o, 1).wait()
            mine = product(p, 2 * o + 1)
            if o == 0:
                acc[p] = mine
            else:
                to_sibling(o, p).wait_recv()
                xs[o - 1, p] = (mine + sr[o, p].astype(jnp.float32)).astype(jnp.bfloat16)
                to_far(o, p).start()

    for p in range(CHUNKS):
        to_sibling(0, p).wait_recv()
        total = acc[p] + sr[0, p].astype(jnp.float32)
        for o in range(1, half):
            to_far(o, p).wait_recv()
            total = total + xr[o - 1, p].astype(jnp.float32)
        out_ref[pl.ds(p * part, part), :] = total.astype(out_ref.dtype)

    @pl.when(z < n - 1)
    def _():
        edge.wait_send()

    for off in range(1, n):

        @pl.when(z + off < n)
        def _(off=off):
            send_state(off).wait_send()

    for p in range(CHUNKS):
        for o in range(half):
            to_sibling(o, p).wait_send()
        for o in range(1, half):
            to_far(o, p).wait_send()


def body(projected, short_filter, decay_rates, residues, skip_gain, out_weight):
    n, m = lax.axis_size("ctx"), lax.axis_size("chan")
    length, width = projected.shape[1:]
    modes = decay_rates.shape[0]
    out_w = out_weight.shape[1] // m
    half = m // 2
    part = length // CHUNKS
    f32, bf16 = jnp.float32, jnp.bfloat16
    table = pltpu.VMEM((modes * SUB, LANES), f32)
    tokens = pltpu.VMEM((length * SUB, LANES), f32)
    dma = pltpu.SemaphoreType.DMA
    vmem = pl.BlockSpec(memory_space=pltpu.VMEM)
    hbm = pl.BlockSpec(memory_space=pl.ANY)
    return pl.pallas_call(
        functools.partial(kernel, n, m),
        out_shape=jax.ShapeDtypeStruct((length, out_w), bf16),
        in_specs=[hbm, vmem, vmem, vmem, vmem, hbm],
        out_specs=vmem,
        scratch_shapes=[
            pltpu.VMEM((3, length, width), bf16),
            pltpu.VMEM((m, width, out_w), bf16),
            pltpu.VMEM((9 * SUB, LANES), f32),
            table,
            table,
            pltpu.VMEM((SUB, LANES), f32),
            table,
            table,
            table,
            table,
            pltpu.VMEM((3, (length + 2) * SUB, LANES), f32),
            tokens,
            tokens,
            tokens,
            pltpu.VMEM((length, width), bf16),
            pltpu.VMEM((modes * SUB, LANES), bf16),
            pltpu.VMEM((n - 1, modes * SUB, LANES), bf16),
            table,
            pltpu.VMEM((half, CHUNKS, part, out_w), bf16),
            pltpu.VMEM((half, CHUNKS, part, out_w), bf16),
            pltpu.VMEM((half - 1, CHUNKS, part, out_w), bf16),
            pltpu.VMEM((half - 1, CHUNKS, part, out_w), bf16),
            pltpu.VMEM((CHUNKS, part, out_w), f32),
            dma,
            dma((m,)),
            dma((2,)),
            dma((n - 1,)),
            dma((n - 1,)),
            dma((half, CHUNKS)),
            dma((half, CHUNKS)),
            dma((half - 1, CHUNKS)),
            dma((half - 1, CHUNKS)),
        ],
        compiler_params=pltpu.CompilerParams(
            collective_id=0, has_side_effects=True, vmem_limit_bytes=48 * 1024 * 1024
        ),
        cost_estimate=pl.CostEstimate(
            flops=2 * length * width * out_w * m, bytes_accessed=2 * width * out_w * m, transcendentals=0
        ),
        name="hyena_layer",
    )(projected, short_filter, decay_rates, residues, skip_gain.reshape(1, width), out_weight)


def solution(mesh):
    in_specs = (
        P(None, ("groups", "ctx"), "chan"),
        P(None, None, "chan"),
        P(None, "chan"),
        P(None, "chan"),
        P("chan"),
        P("chan", None),
    )
    out_specs = P(("groups", "ctx"), "chan")
    return jax.shard_map(body, mesh=mesh, in_specs=in_specs, out_specs=out_specs, check_vma=False)
```

time: 136 us -> 28 us (0.21)
  blocking collectives: 28.1 us -> 0 us
  other arithmetic: 26.2 us -> 0 us
  matrix products: 26.1 us -> 0 us
  Pallas kernels: 0 us -> 20.2 us
  waiting for transfers between devices: 16.2 us -> 0 us
  between operations: 13.6 us -> 0.02 us
  starting transfers between devices: 9.94 us -> 0 us
  local copies, waits for them, and re-layouts: 15.2 us -> 7.46 us
    all_gather x2 -> x0, blocking collectives: 28.1 us -> none  [prefix(): pieces = jax.tree.map(lambda part: lax.all_gather(part, axis), value)]
    dot_general x5 -> x0, matrix products: 26.1 us -> none  [the longest x2 10.9 us: forward_product(): jnp.dot(table, signal, precision=lax.Precision.HIGHEST, preferred_element...]
    pallas_call x0 -> x1, Pallas kernels: none -> 20.2 us  [body(): pl.pallas_call(functools.partial(kernel, n, m), out_shape=jax.ShapeDtypeS...]
    reduce_sum x2 -> x0, other arithmetic: 16.6 us -> none  [the longest x1 9.19 us: body(): filt = jnp.sum(decays * scaled[None, :, :], axis=1)]
    all_gather x1 -> x0, waiting for transfers between devices: 16.2 us -> none  [body(): lax.all_gather(mixed_out, 'chan', axis=1, tiled=True)]
    exp x2 -> x0, other arithmetic: 7.92 us -> none  [the longest x1 7.9 us: body(): decays = jnp.exp(-decay_rates[None, :, :] * offsets[:, None, None])]
    all_to_all x1 -> x0, local copies, waits for them, and re-layouts: 6.21 us -> none  [body(): lax.all_to_all(out_weight, 'chan', split_axis=1, concat_axis=0, tiled=True)]
    all_to_all x1 -> x0, starting transfers between devices: 4.97 us -> none  [body(): lax.all_to_all(out_weight, 'chan', split_axis=1, concat_axis=0, tiled=True)]
  transfers between devices with their start and end apart: 3 -> 0, of which waited for: 1 -> 0; matrix products, arithmetic and copies ran while one was open for 44% -> 0% of each run, Pallas kernels for 0% -> 0%
where the time goes in v1:
time: 28 us; the launch traced here: 27.6 us
  Pallas kernels  20.2 us (72%)
  local copies, waits for them, and re-layouts  7.46 us (27%)
    pallas_call x1, Pallas kernels, body(): pl.pallas_call(functools.partial(kernel, n, m), out_shape=jax.ShapeDtypeS...  20.2 us
    unnamed x13, local copies, waits for them, and re-layouts  7.46 us

profile of v1, /device:TPU:0, one launch (start us, length us, event | category | flops | bytes accessed | tf_op | source)
XLA Modules:
  0.0 27.6 jit_solution(17123598210604954442)
XLA Ops:
  0.0 0.0 copy-start
  0.0 2.2 %copy-done = bf16[1024,2048]{1,0:T(8,128)(2,1)S(1)} copy-done((bf16[1024,2048]{1,0:T(8,128)(2,1)S(1)}, bf16[1024,2048]{1,0:T(8,128)(2,1)}, u32[]{:S(2)}) %copy-start) | copy-done | bytes 4194328
  2.2 0.0 copy-start.1
  2.2 1.4 %copy-done.1 = bf16[3,256,1024]{2,1,0:T(8,128)(2,1)S(1)} copy-done((bf16[3,256,1024]{2,1,0:T(8,128)(2,1)S(1)}, bf16[3,256,1024]{2,1,0:T(8,128)(2,1)}, u32[]{:S(2)}) %copy-start.1) | copy-done | bytes 1572888
  3.6 0.0 copy-start.2
  3.6 0.8 %copy-done.2 = f32[16,1024]{1,0:T(8,128)S(1)} copy-done((f32[16,1024]{1,0:T(8,128)S(1)}, f32[16,1024]{1,0:T(8,128)}, u32[]{:S(2)}) %copy-start.2) | copy-done | bytes 65560
  4.4 0.0 copy-start.3
  4.4 0.8 %copy-done.3 = f32[16,1024]{1,0:T(8,128)S(1)} copy-done((f32[16,1024]{1,0:T(8,128)S(1)}, f32[16,1024]{1,0:T(8,128)}, u32[]{:S(2)}) %copy-start.3) | copy-done | bytes 65560
  5.3 0.0 copy-start.4
  5.3 0.8 %copy-done.4 = f32[3,3,1024]{2,1,0:T(4,128)S(1)} copy-done((f32[3,3,1024]{2,1,0:T(4,128)S(1)}, f32[3,3,1024]{2,1,0:T(4,128)}, u32[]{:S(2)}) %copy-start.4) | copy-done | bytes 36888
  6.1 0.0 copy-start.5
  6.1 0.7 %copy-done.5 = f32[1024]{0:T(1024)S(1)} copy-done((f32[1024]{0:T(1024)S(1)}, f32[1024]{0:T(1024)}, u32[]{:S(2)}) %copy-start.5) | copy-done | bytes 4120
  6.8 20.2 %hyena_layer.1 = bf16[256,512]{1,0:T(8,128)(2,1)S(1)} custom-call(bf16[3,256,1024]{2,1,0:T(8,128)(2,1)S(1)} %copy-done.1, f32[3,3,1024]{2,1,0:T(4,128)S(1)} %copy-done.4, f32[16,1024]{1,0:T(8,128)S(1)} %copy-done.2, f32[16,1024]{1,0:T(8,128)S(1)} %copy-done.3, f32[1,1024]{1,0:T(1,128)S(1)} %bitcast.1, bf16[1024,2048]{1,0:T(8,128)(2,1)S(1)} %copy-done), custom_call_target="tpu_custom_call" | custom-call | flops 1073741824 | bytes 4194304 | tf_op jit(solution)/shard_map/hyena_layer/pallas_call | solution.py:300
  26.9 0.7 %copy.8 = bf16[256,512]{1,0:T(8,128)(2,1)} copy(bf16[256,512]{1,0:T(8,128)(2,1)S(1)} %hyena_layer.1) | data formatting | bytes 524288
Async XLA Ops:
  0.0 2.2 %copy-start = (bf16[1024,2048]{1,0:T(8,128)(2,1)S(1)}, bf16[1024,2048]{1,0:T(8,128)(2,1)}, u32[]{:S(2)}) copy-start(bf16[1024,2048]{1,0:T(8,128)(2,1)} %w_hbm.1) | copy-start | bytes 12582916
  2.2 1.4 %copy-start.1 = (bf16[3,256,1024]{2,1,0:T(8,128)(2,1)S(1)}, bf16[3,256,1024]{2,1,0:T(8,128)(2,1)}, u32[]{:S(2)}) copy-start(bf16[3,256,1024]{2,1,0:T(8,128)(2,1)} %proj_hbm.1) | copy-start | bytes 4718596
  3.6 0.8 %copy-start.2 = (f32[16,1024]{1,0:T(8,128)S(1)}, f32[16,1024]{1,0:T(8,128)}, u32[]{:S(2)}) copy-start(f32[16,1024]{1,0:T(8,128)} %dr_ref.1) | copy-start | bytes 196612
  4.4 0.8 %copy-start.3 = (f32[16,1024]{1,0:T(8,128)S(1)}, f32[16,1024]{1,0:T(8,128)}, u32[]{:S(2)}) copy-start(f32[16,1024]{1,0:T(8,128)} %re_ref.1) | copy-start | bytes 196612
  5.3 0.8 %copy-start.4 = (f32[3,3,1024]{2,1,0:T(4,128)S(1)}, f32[3,3,1024]{2,1,0:T(4,128)}, u32[]{:S(2)}) copy-start(f32[3,3,1024]{2,1,0:T(4,128)} %sf_ref.1) | copy-start | bytes 110596
  6.1 0.7 %copy-start.5 = (f32[1024]{0:T(1024)S(1)}, f32[1024]{0:T(1024)}, u32[]{:S(2)}) copy-start(f32[1024]{0:T(1024)} %param.10) | copy-start | bytes 12292
